TPU v7x, 32 devices: a whole 2x2x4 slice. The times are simulated.
32 devices in a mesh: chain: 2 (over y), gx: 4 (over z), gy: 4 (over x, core).
Axes of the slice: x: 2, y: 2, z: 4, core: 2. Of those that a mesh axis runs over, the one named last changes fastest.
Arguments:
- pressure: float32 [64, 512, 256], P(('chain', 'gx'), 'gy'), parts along dimension 0, may hold values from -3 to 3
- adjoint: float32 [64, 512, 256], P(('chain', 'gx'), 'gy'), parts along dimension 0, may hold values from -3 to 3
- log_perm: float32 [64, 512, 256], P(('chain', 'gx'), 'gy'), parts along dimension 0, may hold values from -3 to 3
- phi_x: float32 [32, 32], P('gx'), may hold values from -1 to 1
- phi_y: float32 [512, 32], P('gy'), may hold values from -0.25 to 0.25
- phi_z: float32 [256, 16], replicated, may hold values from -0.375 to 0.375
- obs_cells: int32 [3, 8192], P(None, 'chain'), parts along dimension 1, may hold values from 0 to 511, as said below
- core_values: float32 [8192], P('chain'), parts along dimension 0, may hold values from -4 to 4
Outputs:
- coeff_grad: float32 [64, 32, 16], P(('chain', 'gx'), 'gy'), parts along dimension 0
There are 2 independent parts, one for each index of `chain`. A program takes and returns all parts, laid end to end along the dimension named above; an argument that names none is the same for every part. Nothing has to cross between parts.
Inputs may be any that keep to these rules, and one draw needn't show every extreme that they name: `obs_cells`: row 0 holds x cells below 32, row 1 y cells below 512, row 2 z cells below 256; cells may repeat.
All inputs are finite; a program needn't handle non-finite values.
Results may differ from a plain program's by a relative error of at most 0.000071.
Values sent between devices are 32-bit elements; how exact they have to be, the bound alone decides.
A program may use at most 64 MiB of HBM per device.

v0:
```python
import jax
import jax.numpy as jnp
from jax import lax
from jax.sharding import PartitionSpec as P

core_weight = 100.0


def padded_2(value, sides, width):
    for axis, dim in sides:
        size, length = (lax.axis_size(axis), value.shape[dim])
        up = [(i, (i + 1) % size) for i in range(size - 1)]
        down = [(j, i) for i, j in up]
        last = lax.slice_in_dim(value, length - width, length, axis=dim)
        first = lax.slice_in_dim(value, 0, width, axis=dim)
        before = lax.ppermute(last, axis, up)
        after = lax.ppermute(first, axis, down)
        value = jnp.concatenate([before, value, after], axis=dim)
    return value


def face_sum(faces, axis_dim):
    count = faces.shape[axis_dim]
    return lax.slice_in_dim(faces, 0, count - 1, axis=axis_dim) + lax.slice_in_dim(
        faces, 1, count, axis=axis_dim
    )


def face_mask(count, index, shard, total):
    global_face = index * shard + jnp.arange(count, dtype=jnp.int32)
    return ((global_face >= 1) & (global_face <= total - 1)).astype(jnp.float32)


def body(pressure, adjoint, log_perm, phi_x, phi_y, phi_z, obs_cells, core_values):
    highest = lax.Precision.HIGHEST
    rows, columns, depth = pressure.shape
    row_index = lax.axis_index("gx")
    column_index = lax.axis_index("gy")
    fields = jnp.stack([pressure, adjoint])
    padded = padded_2(fields, (("gx", 1), ("gy", 2)), 1)
    along_x = padded[:, 1:, 1:-1] - padded[:, :-1, 1:-1]
    faces_x = (
        along_x[0]
        * along_x[1]
        * face_mask(rows + 1, row_index, rows, rows * lax.axis_size("gx"))[:, None, None]
    )
    along_y = padded[:, 1:-1, 1:] - padded[:, 1:-1, :-1]
    faces_y = (
        along_y[0]
        * along_y[1]
        * face_mask(columns + 1, column_index, columns, columns * lax.axis_size("gy"))[
            None, :, None
        ]
    )
    along_z = fields[:, :, :, 1:] - fields[:, :, :, :-1]
    zero_plane = jnp.zeros((rows, columns, 1), jnp.float32)
    faces_z = jnp.concatenate([zero_plane, along_z[0] * along_z[1], zero_plane], axis=2)
    face_total = face_sum(faces_x, 0) + face_sum(faces_y, 1) + face_sum(faces_z, 2)
    cell_grad = -0.5 * jnp.exp(log_perm) * face_total
    local_x = obs_cells[0] - row_index * rows
    local_y = obs_cells[1] - column_index * columns
    inside = (local_x >= 0) & (local_x < rows) & (local_y >= 0) & (local_y < columns)
    flat_cell = (local_x * columns + local_y) * depth + obs_cells[2]
    safe_cell = jnp.where(inside, flat_cell, 0)
    cell_count = rows * columns * depth
    misfit = core_weight * (log_perm.reshape(-1)[safe_cell] - core_values)
    target = jnp.where(inside, flat_cell, cell_count)
    cell_grad = cell_grad.reshape(-1).at[target].add(-misfit, mode="drop")
    partial_value = jnp.dot(cell_grad.reshape(-1, depth), phi_z, precision=highest)
    modes_z = phi_z.shape[1]
    partial_value = partial_value.reshape(rows, columns, modes_z)
    partial_value = jnp.einsum("ijz,jb->ibz", partial_value, phi_y, precision=highest)
    modes_x = phi_x.shape[1]
    modes_y = phi_y.shape[1]
    share_x = modes_x // lax.axis_size("gx")
    share_y = modes_y // lax.axis_size("gy")
    summed_rows = lax.psum_scatter(partial_value, "gy", scatter_dimension=1, tiled=True)
    basis = lax.all_to_all(phi_x, "gx", split_axis=1, concat_axis=0, tiled=True)
    piece = lax.all_gather(summed_rows, "gx", axis=0, tiled=True)
    folded = jnp.dot(basis.T, piece.reshape(piece.shape[0], -1), precision=highest)
    return folded.reshape(share_x, share_y, modes_z)


def solution(mesh):
    placed = (
        P(("chain", "gx"), "gy", None),
        P(("chain", "gx"), "gy", None),
        P(("chain", "gx"), "gy", None),
        P("gx", None),
        P("gy", None),
        P(),
        P(None, "chain"),
        P("chain"),
    )
    return jax.shard_map(
        body, mesh=mesh, in_specs=placed, out_specs=P(("chain", "gx"), "gy", None), check_vma=False
    )
```

profile of v0, /device:TPU:0, one launch (start us, length us, event | category | flops | bytes accessed | tf_op | source)
XLA Modules:
  0.0 122.3 jit_solution(7573292597021066252)
XLA Ops:
  6.5 0.0 copy-start
  6.5 0.0 reduce-scatter.2.cloned.1.call-start
  6.5 2.1 %pad_maximum_fusion.9 = (f32[2,1,128,256]{3,2,1,0:T(8,128)}, f32[2,1,128,256]{3,2,1,0:T(8,128)}) fusion(f32[1,8,128,256]{3,2,1,0:T(8,128)} %bitcast.43, f32[1,8,128,256]{3,2,1,0:T(8,128)} %bitcast.48), kind=kLoop, calls=%fused_computation.29 | loop fusion | flops 131072 | bytes 2621440 | tf_op jit(solution)/shard_map/slice | solution.py:14
  8.6 1.4 %collective-permute-start = (f32[2,1,128,256]{3,2,1,0:T(8,128)}, f32[2,1,128,256]{3,2,1,0:T(8,128)S(1)}, u32[]{:S(2)}, u32[]{:S(2)}) collective-permute-start(f32[2,1,128,256]{3,2,1,0:T(8,128)} %get-tuple-element.11), channel_id=1, source_target_pairs={{4,0},{8,4},{12,8},{5,1},{9,5},{13,9},{6,2},{10,6},{14,10},{7,3},{... | collective-permute-start | bytes 786440 | tf_op jit(solution)/shard_map/ppermute | solution.py:17
  10.1 6.3 %collective-permute-start.1 = (f32[2,1,128,256]{3,2,1,0:T(8,128)}, f32[2,1,128,256]{3,2,1,0:T(8,128)}, u32[]{:S(2)}, u32[]{:S(2)}) collective-permute-start(f32[2,1,128,256]{3,2,1,0:T(8,128)} %get-tuple-element.10), channel_id=1, source_target_pairs={{0,4},{4,8},{8,12},{1,5},{5,9},{9,13},{2,6},{6,10},{10,14},{3,7},{... | collective-permute-start | bytes 786440 | tf_op jit(solution)/shard_map/ppermute | solution.py:16
  16.3 0.0 copy-done.2
  16.3 0.0 copy-done.1
  16.3 1.9 %fusion.1 = f32[2,8,128,255]{3,2,1,0:T(8,128)} fusion(f32[1,8,128,256]{3,2,1,0:T(8,128)S(1)} %bitcast.44, f32[1,8,128,256]{3,2,1,0:T(8,128)S(1)} %bitcast.49), kind=kLoop, calls=%fused_computation.13 | loop fusion | flops 1566720 | bytes 4186112 | tf_op jit(solution)/shard_map/sub | solution.py:55
  18.3 0.0 copy-done.4
  18.3 0.1 compare_select_fusion
  18.4 1.8 %copy.17 = f32[128,2,8,128]{3,1,2,0:T(2,128)S(1)} copy(f32[128,2,8,128]{3,2,1,0:T(8,128)} %bitcast.53) | data formatting | bytes 2097152
  20.2 0.0 copy-start.5
  20.2 23.0 %gather_fusion = f32[4096]{0:T(1024)S(1)} fusion(f32[262144]{0:T(1024)S(1)} %bitcast.42, s32[4096]{0:T(1024)S(1)} %broadcast_clamp_fusion), kind=kCustom, calls=%fused_computation | custom fusion | bytes 49152 | tf_op jit(solution)/shard_map/gather | solution.py:66
  43.3 1.7 %fusion.6 = f32[8,128,255]{2,1,0:T(8,128)S(1)} fusion(f32[2,8,128,255]{3,2,1,0:T(8,128)} %fusion.1), kind=kLoop, calls=%fused_computation.23 | loop fusion | flops 261120 | bytes 3133440 | tf_op jit(solution)/shard_map/mul | solution.py:57
  45.0 0.0 collective-permute-done
  45.0 0.0 collective-permute-done.1
  45.0 0.8 pad_maximum_fusion.14
  45.8 1.3 %collective-permute-start.2 = (f32[2,10,1,256]{3,2,1,0:T(1,128)S(1)}, f32[2,10,1,256]{3,2,1,0:T(1,128)S(1)}, u32[]{:S(2)}, u32[]{:S(2)}) collective-permute-start(f32[2,10,1,256]{3,2,1,0:T(1,128)S(1)} %get-tuple-element.8), channel_id=1, source_target_pairs={{1,0},{2,1},{3,2},{5,4},{6,5},{7,6},{9,8},{10,9},{11,10},{13,12},{... | collective-permute-start | bytes 61448 | tf_op jit(solution)/shard_map/ppermute | solution.py:17
  47.1 3.0 %collective-permute-start.3 = (f32[2,10,1,256]{3,2,1,0:T(1,128)S(1)}, f32[2,10,1,256]{3,2,1,0:T(1,128)S(1)}, u32[]{:S(2)}, u32[]{:S(2)}) collective-permute-start(f32[2,10,1,256]{3,2,1,0:T(1,128)S(1)} %get-tuple-element.9), channel_id=1, source_target_pairs={{0,1},{1,2},{2,3},{4,5},{5,6},{6,7},{8,9},{9,10},{10,11},{12,13},{... | collective-permute-start | bytes 61448 | tf_op jit(solution)/shard_map/ppermute | solution.py:16
  50.1 1.1 maximum_subtract_fusion
  51.3 0.2 fusion.3
  51.5 0.0 collective-permute-done.2
  51.5 0.0 collective-permute-done.3
  51.5 0.2 fusion
  51.8 0.0 copy-start.3
  51.8 0.2 fusion.5
  51.9 1.1 copy-done.3
  53.0 0.5 fusion.9
  53.5 0.5 copy.16
  54.1 22.8 %scatter_fusion = f32[262144]{0:T(1024)S(1)} fusion(f32[262144]{0:T(1024)S(1)} %bitcast.41, s32[4096]{0:T(1024)S(1)} %bitcast.56, f32[4096]{0:T(1024)S(1)} %multiply_negate_fusion), kind=kCustom, calls=%fused_computation.1 | custom fusion | flops 4096 | bytes 65536 | tf_op jit(solution)/shard_map/scatter-add | solution.py:68
  76.9 0.0 copy-start.6
  76.9 0.0 copy-start.7
  76.9 0.3 dot_general.13
  77.2 0.0 copy-done
  77.2 1.0 fusion.11
  78.2 0.0 copy-done.6
  78.2 0.2 convolution_bitcast_fusion
  78.4 0.8 copy.11
  79.2 0.0 reduce-scatter.2.cloned.1.call-update
  79.2 0.1 copy.14
  79.3 9.0 %all_to_all.19 = f32[8,4,8]{0,2,1:T(8,128)S(1)} all-to-all(f32[8,4,8]{0,2,1:T(8,128)S(1)} %bitcast.58), channel_id=1, replica_groups=mesh['chain'=2,'gx'=4,'gy'=4] {'gx'}, dimensions={1} | all-to-all | bytes 2048 | tf_op jit(solution)/shard_map/all_to_all | solution.py:78
  88.3 0.1 all_to_all.17
  88.4 11.8 %reduce-scatter.2.cloned.1.call-done = f32[8,8,16]{2,0,1:T(8,128)} async-done(((f32[8,32,16]{2,0,1:T(8,128)}), f32[8,8,16]{2,0,1:T(8,128)}) %reduce-scatter.2.cloned.1.call-update) | async-done | bytes 4112 | tf_op jit(solution)/shard_map/reduce_scatter | solution.py:77
  100.2 0.8 copy.12
  101.0 13.4 %all_gather.3 = f32[32,8,16]{2,1,0:T(8,128)S(1)} all-gather(f32[8,8,16]{2,1,0:T(8,128)S(1)} %copy.12), channel_id=1, replica_groups=mesh['chain'=2,'gx'=4,'gy'=4] {'gx'}, dimensions={0}, use_global_device_ids=true | all-gather | bytes 20480 | tf_op jit(solution)/shard_map/all_gather | solution.py:79
  114.4 0.1 copy.13
  114.5 0.2 convolution_bitcast_fusion.1
  114.7 0.7 reshape.156
  (11 shorter events, 0.1 us)
Async XLA Ops:
  6.5 70.7 %copy-start = (f32[256,16]{0,1:T(8,128)S(1)}, f32[256,16]{0,1:T(8,128)}, u32[]{:S(2)}) copy-start(f32[256,16]{0,1:T(8,128)} %param.13) | copy-start | bytes 49156
  6.5 9.8 %copy-start.2 = (f32[8,128,256]{2,1,0:T(8,128)S(1)}, f32[8,128,256]{2,1,0:T(8,128)}, u32[]{:S(2)}) copy-start(f32[8,128,256]{2,1,0:T(8,128)} %param.8) | copy-start | bytes 3145732
  6.5 9.8 %copy-start.1 = (f32[8,128,256]{2,1,0:T(8,128)S(1)}, f32[8,128,256]{2,1,0:T(8,128)}, u32[]{:S(2)}) copy-start(f32[8,128,256]{2,1,0:T(8,128)} %param.9) | copy-start | bytes 3145732
  6.5 93.7 %reduce-scatter.2.cloned.1.call-start = ((), (), s32[]{:S(2)}) async-start(), calls=%async_computation.2 | async-start | bytes 163840 | tf_op jit(solution)/shard_map/reduce_scatter | solution.py:77
  8.6 9.7 %copy-start.4 = (s32[3,4096]{1,0:T(4,128)S(1)}, s32[3,4096]{1,0:T(4,128)}, u32[]{:S(2)}) copy-start(s32[3,4096]{1,0:T(4,128)} %param.14) | copy-start | bytes 147460
  8.6 36.4 %collective-permute-start = (f32[2,1,128,256]{3,2,1,0:T(8,128)}, f32[2,1,128,256]{3,2,1,0:T(8,128)S(1)}, u32[]{:S(2)}, u32[]{:S(2)}) collective-permute-start(f32[2,1,128,256]{3,2,1,0:T(8,128)} %get-tuple-element.11), channel_id=1, source_target_pairs={{4,0},{8,4},{12,8},{5,1},{9,5},{13,9},{6,2},{10,6},{14,10},{7,3},{... | collective-permute-start | bytes 786440 | tf_op jit(solution)/shard_map/ppermute | solution.py:17
  10.1 34.9 %collective-permute-start.1 = (f32[2,1,128,256]{3,2,1,0:T(8,128)}, f32[2,1,128,256]{3,2,1,0:T(8,128)}, u32[]{:S(2)}, u32[]{:S(2)}) collective-permute-start(f32[2,1,128,256]{3,2,1,0:T(8,128)} %get-tuple-element.10), channel_id=1, source_target_pairs={{0,4},{4,8},{8,12},{1,5},{5,9},{9,13},{2,6},{6,10},{10,14},{3,7},{... | collective-permute-start | bytes 786440 | tf_op jit(solution)/shard_map/ppermute | solution.py:16
  20.2 23.1 %copy-start.5 = (f32[4096]{0:T(1024)S(1)}, f32[4096]{0:T(1024)}, u32[]{:S(2)}) copy-start(f32[4096]{0:T(1024)} %param.15) | copy-start | bytes 49156
  45.8 5.7 %collective-permute-start.2 = (f32[2,10,1,256]{3,2,1,0:T(1,128)S(1)}, f32[2,10,1,256]{3,2,1,0:T(1,128)S(1)}, u32[]{:S(2)}, u32[]{:S(2)}) collective-permute-start(f32[2,10,1,256]{3,2,1,0:T(1,128)S(1)} %get-tuple-element.8), channel_id=1, source_target_pairs={{1,0},{2,1},{3,2},{5,4},{6,5},{7,6},{9,8},{10,9},{11,10},{13,12},{... | collective-permute-start | bytes 61448 | tf_op jit(solution)/shard_map/ppermute | solution.py:17
  47.1 4.4 %collective-permute-start.3 = (f32[2,10,1,256]{3,2,1,0:T(1,128)S(1)}, f32[2,10,1,256]{3,2,1,0:T(1,128)S(1)}, u32[]{:S(2)}, u32[]{:S(2)}) collective-permute-start(f32[2,10,1,256]{3,2,1,0:T(1,128)S(1)} %get-tuple-element.9), channel_id=1, source_target_pairs={{0,1},{1,2},{2,3},{4,5},{5,6},{6,7},{8,9},{9,10},{10,11},{12,13},{... | collective-permute-start | bytes 61448 | tf_op jit(solution)/shard_map/ppermute | solution.py:16
  51.8 1.2 %copy-start.3 = (f32[8,128,256]{2,1,0:T(8,128)S(1)}, f32[8,128,256]{2,1,0:T(8,128)}, u32[]{:S(2)}) copy-start(f32[8,128,256]{2,1,0:T(8,128)} %param.10) | copy-start | bytes 3145732
  76.9 1.3 %copy-start.6 = (f32[128,32]{0,1:T(8,128)S(1)}, f32[128,32]{0,1:T(8,128)}, u32[]{:S(2)}) copy-start(f32[128,32]{0,1:T(8,128)} %param.12) | copy-start | bytes 49156
  76.9 2.3 %copy-start.7 = (f32[8,32]{1,0:T(8,128)S(1)}, f32[8,32]{1,0:T(8,128)}, u32[]{:S(2)}) copy-start(f32[8,32]{1,0:T(8,128)} %param.11) | copy-start | bytes 3076
Sparse Core Ops, SparseCore 0:
  79.3 20.8 reduce-scatter.1
where the time goes:
time: 123 us; the launch traced here: 122 us
  other arithmetic  31.7 us (26%)
  local copies, waits for them, and re-layouts  29.2 us (24%)
  blocking collectives  22.4 us (18%)
  between operations  13.6 us (11%)
  starting transfers between devices  12 us (10%)
  waiting for transfers between devices  11.9 us (10%)
  matrix products  1.37 us (1%)
    gather x1, local copies, waits for them, and re-layouts, body(): misfit = core_weight * (log_perm.reshape(-1)[safe_cell] - core_values)  23 us
    scatter-add x1, other arithmetic, body(): cell_grad = cell_grad.reshape(-1).at[target].add(-misfit, mode='drop')  22.8 us
    all_gather x1, blocking collectives, body(): piece = lax.all_gather(summed_rows, 'gx', axis=0, tiled=True)  13.4 us
    reduce_scatter x1, waiting for transfers between devices, body(): lax.psum_scatter(partial_value, 'gy', scatter_dimension=1, tiled=True)  11.8 us
    ppermute x2, starting transfers between devices, padded_2(): before = lax.ppermute(last, axis, up)  9.31 us
    all_to_all x1, blocking collectives, body(): basis = lax.all_to_all(phi_x, 'gx', split_axis=1, concat_axis=0, tiled=True)  9.02 us
    unnamed x19, local copies, waits for them, and re-layouts  3.48 us
    ppermute x2, starting transfers between devices, padded_2(): after = lax.ppermute(first, axis, down)  2.7 us
  transfers between devices with their start and end apart: 5, of which 1 were waited for; matrix products, arithmetic and copies ran while one was open for 25% of the time, Pallas kernels for 0%

commit v1 on v0

v1 whole, which is shorter than its diff:
```python
import functools

import jax
import jax.numpy as jnp
from jax import lax
from jax.experimental import pallas as pl
from jax.experimental.pallas import tpu as pltpu
from jax.sharding import PartitionSpec as P

core_weight = 100.0
TILE = 8
CHUNK = 512
f32, bf16 = jnp.float32, jnp.bfloat16
MESH = pl.DeviceIdType.MESH


def dot_nn(a, b):
    return lax.dot_general(a, b, (((1,), (0,)), ((), ())), preferred_element_type=f32)


def dot_nt(a, b):
    return lax.dot_general(a, b, (((1,), (1,)), ((), ())), preferred_element_type=f32)


def split(value):
    high = value.astype(bf16)
    return high, (value - high.astype(f32)).astype(bf16)


def one_hot(size, width, which):
    return jnp.where(lax.broadcasted_iota(jnp.int32, (size, width), 0) == which, 1.0, 0.0)


def each(count, step):
    if count <= 16:
        for i in range(count):
            step(i)
    else:
        lax.fori_loop(0, count, lambda i, c: (step(i), c)[1], 0)


def stacked(value):
    return jnp.concatenate(split(value), axis=0)


def kernel(
    n_gx, n_gy,
    p_in, a_in, lp_in, phix_in, phiy_in, phiz_in, obs_in, core_in,
    out_ref,
    p, a, lp, phix, phiy, phiz, obs, core,
    counts, cores, part, kron, pieces, landed,
    load_sems, halo_send, halo_recv, piece_send, piece_recv,
):
    rows, cols, depth = lp.shape
    mx, my, mz = phix.shape[1], phiy.shape[0], phiz.shape[0]
    share_x, share_y = mx // n_gx, my // n_gy
    width = share_x * mz
    gx, gy = lax.axis_index("gx"), lax.axis_index("gy")
    peers = n_gx * n_gy

    def peer(d):
        return lax.rem(gx + d // n_gy, n_gx), lax.rem(gy + d % n_gy, n_gy)

    barrier = pltpu.get_barrier_semaphore()

    def greet(d):
        tx, ty = peer(d + 1)
        pl.semaphore_signal(barrier, inc=1, device_id={"gx": tx, "gy": ty}, device_id_type=MESH)

    each(peers - 1, greet)

    inner = (pl.ds(1, rows), pl.ds(TILE, cols))
    loads = [
        pltpu.make_async_copy(src, dst, load_sems.at[i])
        for i, (src, dst) in enumerate(
            (
                (obs_in, obs),
                (core_in, core),
                (phix_in, phix),
                (phiy_in, phiy),
                (phiz_in, phiz),
                (p_in, p.at[inner]),
                (a_in, a.at[inner]),
                (lp_in, lp),
            )
        )
    ]
    for load in loads:
        load.start()

    pl.semaphore_wait(barrier, peers - 1)

    own_cols = pl.ds(TILE, cols)
    own_rows = pl.ds(1, rows)

    def halo(k, field, array, scratch):
        src, dst, target = (
            (array.at[rows - 1], scratch.at[0, own_cols], {"gx": gx + 1}),
            (array.at[0], scratch.at[rows + 1, own_cols], {"gx": gx - 1}),
            (
                array.at[:, pl.ds(cols - TILE, TILE)],
                scratch.at[own_rows, pl.ds(0, TILE)],
                {"gy": gy + 1},
            ),
            (
                array.at[:, pl.ds(0, TILE)],
                scratch.at[own_rows, pl.ds(cols + TILE, TILE)],
                {"gy": gy - 1},
            ),
        )[k]
        return pltpu.make_async_remote_copy(
            src_ref=src,
            dst_ref=dst,
            send_sem=halo_send.at[2 * k + field],
            recv_sem=halo_recv.at[2 * k + field],
            device_id=target,
            device_id_type=MESH,
        )

    fields = ((0, p_in, p), (1, a_in, a))
    sends = (gx < n_gx - 1, gx > 0, gy < n_gy - 1, gy > 0)
    gets = (gx > 0, gx < n_gx - 1, gy > 0, gy < n_gy - 1)
    for k in (0, 1, 2, 3):

        @pl.when(sends[k])
        def _(k=k):
            for field, array, scratch in fields:
                halo(k, field, array, scratch).start()

    for load in loads[:5]:
        load.wait()

    phiz_t = stacked(phiz[...])
    phiy_t = stacked(phiy[...])
    counts[...] = jnp.zeros_like(counts)
    cores[...] = jnp.zeros_like(cores)

    def observe(c, carry):
        at = pl.ds(pl.multiple_of(c * CHUNK, CHUNK), CHUNK)
        local_x = obs[0:1, at] - gx * rows
        in_y = one_hot(cols, CHUNK, obs[1:2, at] - gy * cols).astype(bf16)
        in_z = one_hot(depth, CHUNK, obs[2:3, at]).astype(bf16)
        in_x = [jnp.where(local_x == i, 1.0, 0.0).astype(bf16) for i in range(rows)]
        cells = jnp.concatenate([in_y * in_x[i] for i in range(rows)], axis=0)
        counts[...] += dot_nt(cells, in_z)
        both = dot_nn(phiz_t, in_z)
        high, low = split((both[:mz] + both[mz:]) * core[0:1, at])
        weighted = jnp.concatenate(
            [high * in_x[i] for i in range(rows)] + [low * in_x[i] for i in range(rows)], axis=0
        )
        cores[...] += dot_nt(weighted, in_y)
        return carry

    lax.fori_loop(0, obs.shape[1] // CHUNK, observe, 0)

    tall, wide = rows * mz, mx * mz
    spread_rows = jnp.where(
        lax.broadcasted_iota(jnp.int32, (tall, rows), 0) // mz
        == lax.broadcasted_iota(jnp.int32, (tall, rows), 1),
        1.0,
        0.0,
    ).astype(bf16)
    spread_cols = jnp.where(
        lax.broadcasted_iota(jnp.int32, (mx, wide), 1) // mz
        == lax.broadcasted_iota(jnp.int32, (mx, wide), 0),
        1.0,
        0.0,
    ).astype(bf16)
    same = lax.rem(lax.broadcasted_iota(jnp.int32, (tall, wide), 0), mz) == lax.rem(
        lax.broadcasted_iota(jnp.int32, (tall, wide), 1), mz
    )
    for i, half in enumerate(split(phix[...])):
        block = dot_nn(dot_nn(spread_rows, half).astype(bf16), spread_cols)
        kron[i] = jnp.where(same, block, 0.0).astype(bf16)

    for load in loads[5:]:
        load.wait()

    for k in (2, 3):
        @pl.when(gets[k])
        def _(k=k):
            for field, array, scratch in fields:
                halo(k, field, array, scratch).wait_recv()

        @pl.when(jnp.logical_not(gets[k]))
        def _(k=k):
            for _, _, scratch in fields:
                line = TILE if k == 2 else TILE + cols - 1
                place = 0 if k == 2 else TILE + cols
                for i in range(1, rows + 1):
                    scratch[i, place : place + TILE] = jnp.broadcast_to(
                        scratch[i, line : line + 1], (TILE, depth)
                    )

    def own(scratch, i):
        return scratch[i, TILE : TILE + cols]

    last = lax.broadcasted_iota(jnp.int32, (cols, depth), 1) == depth - 1

    def flat_faces(i):
        pc, ac = own(p, i), own(a, i)
        up = (pltpu.roll(pc, depth - 1, 1) - pc) * (pltpu.roll(ac, depth - 1, 1) - ac)
        up = jnp.where(last, 0.0, up)
        total = up + pltpu.roll(up, 1, 1)
        for s in (TILE - 1, TILE + 1):
            total += (p[i, s : s + cols] - pc) * (a[i, s : s + cols] - ac)
        return total

    def x_face(i, j):
        return (own(p, i) - own(p, j)) * (own(a, i) - own(a, j))

    def project(i, total):
        field = lp[i]
        cell = -0.5 * jnp.exp(field) * total - (core_weight * counts[i * cols : (i + 1) * cols]) * field
        high, low = split(cell)
        x = dot_nt(phiz_t, high)
        x = x[:mz] + x[mz:] + dot_nt(phiz_t[:mz], low)
        at = pl.ds(i * mz, mz)
        top = i * mz
        seen = cores[top : top + mz] + cores[tall + top : tall + top + mz]
        part[at] = x + core_weight * seen

    for i in range(1, rows - 1):
        project(i, flat_faces(i + 1) + x_face(i + 1, i) + x_face(i + 1, i + 2))
    edges = [flat_faces(1) + x_face(1, 2), flat_faces(rows) + x_face(rows, rows - 1)]

    for k in (0, 1):

        @pl.when(gets[k])
        def _(k=k):
            for field, array, scratch in fields:
                halo(k, field, array, scratch).wait_recv()

        @pl.when(jnp.logical_not(gets[k]))
        def _(k=k):
            for _, _, scratch in fields:
                scratch[(rows + 1) * k, TILE : TILE + cols] = own(scratch, 1 + (rows - 1) * k)

    project(0, edges[0] + x_face(1, 0))
    project(rows - 1, edges[1] + x_face(rows, rows + 1))

    high, low = split(part[...])
    y = dot_nt(phiy_t, high)
    y = y[:my] + y[my:] + dot_nt(phiy_t[:my], low)
    high, low = split(y)
    folded = dot_nn(high, kron[0]) + dot_nn(low, kron[0]) + dot_nn(high, kron[1])
    for i in range(n_gx):
        for j in range(n_gy):
            pieces[i, j] = folded[j * share_y : (j + 1) * share_y, i * width : (i + 1) * width]

    def piece(d):
        tx, ty = peer(d)
        return pltpu.make_async_remote_copy(
            src_ref=pieces.at[tx, ty],
            dst_ref=landed.at[d],
            send_sem=piece_send,
            recv_sem=piece_recv,
            device_id={"gx": tx, "gy": ty},
            device_id_type=MESH,
        )

    each(peers - 1, lambda d: piece(d + 1).start())
    landed[0] = pieces[gx, gy]
    rest = landed.at[pl.ds(1, peers - 1)]
    pltpu.make_async_copy(rest, rest, piece_recv).wait()
    out_ref[...] = jnp.sum(landed[...], axis=0)
    pltpu.make_async_copy(rest, rest, piece_send).wait()
    for k in (0, 1, 2, 3):

        @pl.when(sends[k])
        def _(k=k):
            for field, array, scratch in fields:
                halo(k, field, array, scratch).wait_send()


def body(pressure, adjoint, log_perm, phi_x, phi_y, phi_z, obs_cells, core_values):
    rows, cols, depth = pressure.shape
    n_gx, n_gy = lax.axis_size("gx"), lax.axis_size("gy")
    mx, my, mz = phi_x.shape[1], phi_y.shape[1], phi_z.shape[1]
    share_x, share_y = mx // n_gx, my // n_gy
    width = share_x * mz
    seen = core_values.shape[0]
    padded = (rows + 2, cols + 2 * TILE, depth)
    phi_y, phi_z = phi_y.T, phi_z.T
    cores = core_values.reshape(1, seen)
    args = (pressure, adjoint, log_perm, phi_x, phi_y, phi_z, obs_cells, cores)
    out = pl.pallas_call(
        functools.partial(kernel, n_gx, n_gy),
        out_shape=jax.ShapeDtypeStruct((share_y, width), f32),
        in_specs=[pl.BlockSpec(memory_space=pltpu.HBM)] * len(args),
        out_specs=pl.BlockSpec(memory_space=pltpu.VMEM),
        scratch_shapes=[
            pltpu.VMEM(padded, f32),
            pltpu.VMEM(padded, f32),
            pltpu.VMEM((rows, cols, depth), f32),
            pltpu.VMEM(phi_x.shape, f32),
            pltpu.VMEM(phi_y.shape, f32),
            pltpu.VMEM(phi_z.shape, f32),
            pltpu.VMEM(obs_cells.shape, jnp.int32),
            pltpu.VMEM((1, seen), f32),
            pltpu.VMEM((rows * cols, depth), f32),
            pltpu.VMEM((2 * rows * mz, cols), f32),
            pltpu.VMEM((rows * mz, cols), f32),
            pltpu.VMEM((2, rows * mz, mx * mz), bf16),
            pltpu.VMEM((n_gx, n_gy, share_y, width), f32),
            pltpu.VMEM((n_gx * n_gy, share_y, width), f32),
            pltpu.SemaphoreType.DMA((8,)),
            pltpu.SemaphoreType.DMA((8,)),
            pltpu.SemaphoreType.DMA((8,)),
            pltpu.SemaphoreType.DMA,
            pltpu.SemaphoreType.DMA,
        ],
        compiler_params=pltpu.CompilerParams(
            collective_id=0, has_side_effects=True, vmem_limit_bytes=63 * 1024 * 1024
        ),
    )(*args)
    return out.reshape(share_y, share_x, mz).transpose(1, 0, 2)


def solution(mesh):
    placed = (
        P(("chain", "gx"), "gy", None),
        P(("chain", "gx"), "gy", None),
        P(("chain", "gx"), "gy", None),
        P("gx", None),
        P("gy", None),
        P(),
        P(None, "chain"),
        P("chain"),
    )
    return jax.shard_map(
        body, mesh=mesh, in_specs=placed, out_specs=P(("chain", "gx"), "gy", None), check_vma=False
    )
```

time: 123 us -> 19.9 us (0.16)
  other arithmetic: 31.7 us -> 0 us
  local copies, waits for them, and re-layouts: 29.2 us -> 1.38 us
  blocking collectives: 22.4 us -> 0 us
  Pallas kernels: 0 us -> 18.3 us
  between operations: 13.6 us -> 0.01 us
  starting transfers between devices: 12 us -> 0 us
  waiting for transfers between devices: 11.9 us -> 0 us
  matrix products: 1.37 us -> 0 us
    gather x1 -> x0, local copies, waits for them, and re-layouts: 23 us -> none  [body(): misfit = core_weight * (log_perm.reshape(-1)[safe_cell] - core_values)]
    scatter-add x1 -> x0, other arithmetic: 22.8 us -> none  [body(): cell_grad = cell_grad.reshape(-1).at[target].add(-misfit, mode='drop')]
    pallas_call x0 -> x1, Pallas kernels: none -> 18.3 us  [body(): pl.pallas_call(functools.partial(kernel, n_gx, n_gy), out_shape=jax.Shape...]
    all_gather x1 -> x0, blocking collectives: 13.4 us -> none  [body(): piece = lax.all_gather(summed_rows, 'gx', axis=0, tiled=True)]
    ppermute x4 -> x0, starting transfers between devices: 12 us -> none  [the longest x2 9.31 us: padded_2(): before = lax.ppermute(last, axis, up)]
    reduce_scatter x1 -> x0, waiting for transfers between devices: 11.8 us -> none  [body(): lax.psum_scatter(partial_value, 'gy', scatter_dimension=1, tiled=True)]
    all_to_all x1 -> x0, blocking collectives: 9.02 us -> none  [body(): basis = lax.all_to_all(phi_x, 'gx', split_axis=1, concat_axis=0, tiled=True)]
    unnamed x19 -> x0, local copies, waits for them, and re-layouts: 3.48 us -> none
  transfers between devices with their start and end apart: 5 -> 0, of which waited for: 1 -> 0; matrix products, arithmetic and copies ran while one was open for 25% -> 0% of each run, Pallas kernels for 0% -> 0%
where the time goes in v1:
time: 19.9 us; the launch traced here: 19.7 us
  Pallas kernels  18.3 us (92%)
  local copies, waits for them, and re-layouts  1.38 us (7%)
    pallas_call x1, Pallas kernels, body(): pl.pallas_call(functools.partial(kernel, n_gx, n_gy), out_shape=jax.Shape...  18.3 us
    reshape x2, local copies, waits for them, and re-layouts, body(): return out.reshape(share_y, share_x, mz).transpose(1, 0, 2)  1.38 us

profile of v1, /device:TPU:0, one launch (start us, length us, event | category | flops | bytes accessed | tf_op | source)
XLA Modules:
  0.0 19.7 jit_solution(10067254336357313983)
XLA Ops:
  0.0 18.3 %shard_map.82 = f32[8,128]{1,0:T(8,128)} custom-call(f32[8,128,256]{2,1,0:T(8,128)} %p_in.1, f32[8,128,256]{2,1,0:T(8,128)} %a_in.1, f32[8,128,256]{2,1,0:T(8,128)} %lp_in.1, f32[8,32]{1,0:T(8,128)} %phix_in.1, f32[32,128]{1,0:T(8,128)} %bitcast.6, f32[16,256]{1,0:T(8,128)} %bitcast.7, s32[3,4096]{1,0:T(4,128)} %obs_in.1, f32[1,4096]{1,0:T(1,128)} %bitcast.8), custom_call_target="tpu_custom_call" | custom-call | tf_op jit(solution)/shard_map/pallas_call | solution.py:287
  18.4 0.8 %reshape.7 = f32[8,8,16]{2,1,0:T(8,128)S(1)} reshape(f32[8,128]{1,0:T(8,128)} %shard_map.82) | data formatting | bytes 8192 | tf_op jit(solution)/shard_map/reshape | solution.py:317
  19.1 0.6 %copy.11 = f32[8,8,16]{2,0,1:T(8,128)} copy(f32[8,8,16]{2,1,0:T(8,128)S(1)} %reshape.7) | data formatting | bytes 8192 | tf_op jit(solution)/shard_map/reshape | solution.py:317

commit v2 on v1

--- a/solution.py
+++ b/solution.py
@@ -48,8 +48,8 @@
     p_in, a_in, lp_in, phix_in, phiy_in, phiz_in, obs_in, core_in,
     out_ref,
     p, a, lp, phix, phiy, phiz, obs, core,
-    counts, cores, part, kron, pieces, landed,
-    load_sems, halo_send, halo_recv, piece_send, piece_recv,
+    counts, cores, part, kron, leave, arrive, pieces, landed,
+    load_sems, halo_send, halo_recv, piece_send, piece_recv, ready,
 ):
     rows, cols, depth = lp.shape
     mx, my, mz = phix.shape[1], phiy.shape[0], phiz.shape[0]
@@ -61,98 +61,34 @@
     def peer(d):
         return lax.rem(gx + d // n_gy, n_gx), lax.rem(gy + d % n_gy, n_gy)
 
-    barrier = pltpu.get_barrier_semaphore()
-
-    def greet(d):
-        tx, ty = peer(d + 1)
-        pl.semaphore_signal(barrier, inc=1, device_id={"gx": tx, "gy": ty}, device_id_type=MESH)
-
-    each(peers - 1, greet)
-
     inner = (pl.ds(1, rows), pl.ds(TILE, cols))
     loads = [
         pltpu.make_async_copy(src, dst, load_sems.at[i])
         for i, (src, dst) in enumerate(
             (
+                (phix_in, phix),
+                (p_in, p.at[inner]),
+                (a_in, a.at[inner]),
+                (phiy_in, phiy),
+                (phiz_in, phiz),
                 (obs_in, obs),
                 (core_in, core),
-                (phix_in, phix),
-                (phiy_in, phiy),
-                (phiz_in, phiz),
-                (p_in, p.at[inner]),
-                (a_in, a.at[inner]),
                 (lp_in, lp),
             )
         )
     ]
+    barrier = pltpu.get_barrier_semaphore()
+
+    def signal(semaphore, axis, size, d):
+        target = {axis: lax.rem(lax.axis_index(axis) + d + 1, size)}
+        pl.semaphore_signal(semaphore, inc=1, device_id=target, device_id_type=MESH)
+
+    each(n_gx - 1, functools.partial(signal, barrier, "gx", n_gx))
+    each(n_gy - 1, functools.partial(signal, barrier, "gy", n_gy))
     for load in loads:
         load.start()
 
-    pl.semaphore_wait(barrier, peers - 1)
-
-    own_cols = pl.ds(TILE, cols)
-    own_rows = pl.ds(1, rows)
-
-    def halo(k, field, array, scratch):
-        src, dst, target = (
-            (array.at[rows - 1], scratch.at[0, own_cols], {"gx": gx + 1}),
-            (array.at[0], scratch.at[rows + 1, own_cols], {"gx": gx - 1}),
-            (
-                array.at[:, pl.ds(cols - TILE, TILE)],
-                scratch.at[own_rows, pl.ds(0, TILE)],
-                {"gy": gy + 1},
-            ),
-            (
-                array.at[:, pl.ds(0, TILE)],
-                scratch.at[own_rows, pl.ds(cols + TILE, TILE)],
-                {"gy": gy - 1},
-            ),
-        )[k]
-        return pltpu.make_async_remote_copy(
-            src_ref=src,
-            dst_ref=dst,
-            send_sem=halo_send.at[2 * k + field],
-            recv_sem=halo_recv.at[2 * k + field],
-            device_id=target,
-            device_id_type=MESH,
-        )
-
-    fields = ((0, p_in, p), (1, a_in, a))
-    sends = (gx < n_gx - 1, gx > 0, gy < n_gy - 1, gy > 0)
-    gets = (gx > 0, gx < n_gx - 1, gy > 0, gy < n_gy - 1)
-    for k in (0, 1, 2, 3):
-
-        @pl.when(sends[k])
-        def _(k=k):
-            for field, array, scratch in fields:
-                halo(k, field, array, scratch).start()
-
-    for load in loads[:5]:
-        load.wait()
-
-    phiz_t = stacked(phiz[...])
-    phiy_t = stacked(phiy[...])
-    counts[...] = jnp.zeros_like(counts)
-    cores[...] = jnp.zeros_like(cores)
-
-    def observe(c, carry):
-        at = pl.ds(pl.multiple_of(c * CHUNK, CHUNK), CHUNK)
-        local_x = obs[0:1, at] - gx * rows
-        in_y = one_hot(cols, CHUNK, obs[1:2, at] - gy * cols).astype(bf16)
-        in_z = one_hot(depth, CHUNK, obs[2:3, at]).astype(bf16)
-        in_x = [jnp.where(local_x == i, 1.0, 0.0).astype(bf16) for i in range(rows)]
-        cells = jnp.concatenate([in_y * in_x[i] for i in range(rows)], axis=0)
-        counts[...] += dot_nt(cells, in_z)
-        both = dot_nn(phiz_t, in_z)
-        high, low = split((both[:mz] + both[mz:]) * core[0:1, at])
-        weighted = jnp.concatenate(
-            [high * in_x[i] for i in range(rows)] + [low * in_x[i] for i in range(rows)], axis=0
-        )
-        cores[...] += dot_nt(weighted, in_y)
-        return carry
-
-    lax.fori_loop(0, obs.shape[1] // CHUNK, observe, 0)
-
+    loads[0].wait()
     tall, wide = rows * mz, mx * mz
     spread_rows = jnp.where(
         lax.broadcasted_iota(jnp.int32, (tall, rows), 0) // mz
@@ -172,25 +108,84 @@
     for i, half in enumerate(split(phix[...])):
         block = dot_nn(dot_nn(spread_rows, half).astype(bf16), spread_cols)
         kron[i] = jnp.where(same, block, 0.0).astype(bf16)
-
-    for load in loads[5:]:
-        load.wait()
-
-    for k in (2, 3):
-        @pl.when(gets[k])
+    loads[1].wait()
+    loads[2].wait()
+    for field, scratch in ((0, p), (1, a)):
+        leave[0, field] = scratch[1 : rows + 1, TILE + cols - 1]
+        leave[1, field] = scratch[1 : rows + 1, TILE]
+
+    pl.semaphore_wait(barrier, n_gx + n_gy - 2)
+
+    own_cols = pl.ds(TILE, cols)
+
+    def halo(k, field, array, scratch):
+        src, dst, target = (
+            (array.at[rows - 1], scratch.at[0, own_cols], {"gx": gx + 1}),
+            (array.at[0], scratch.at[rows + 1, own_cols], {"gx": gx - 1}),
+            (leave.at[0, field], arrive.at[0, field], {"gy": gy + 1}),
+            (leave.at[1, field], arrive.at[1, field], {"gy": gy - 1}),
+        )[k]
+        return pltpu.make_async_remote_copy(
+            src_ref=src,
+            dst_ref=dst,
+            send_sem=halo_send.at[2 * k + field],
+            recv_sem=halo_recv.at[2 * k + field],
+            device_id=target,
+            device_id_type=MESH,
+        )
+
+    fields = ((0, p_in, p), (1, a_in, a))
+    sends = (gx < n_gx - 1, gx > 0, gy < n_gy - 1, gy > 0)
+    gets = (gx > 0, gx < n_gx - 1, gy > 0, gy < n_gy - 1)
+    for k in (0, 1, 2, 3):
+
+        @pl.when(sends[k])
         def _(k=k):
             for field, array, scratch in fields:
+                halo(k, field, array, scratch).start()
+
+    each(n_gx - 1, functools.partial(signal, ready, "gx", n_gx))
+    for load in loads[3:7]:
+        load.wait()
+
+    phiz_t = stacked(phiz[...])
+    phiy_t = stacked(phiy[...])
+    counts[...] = jnp.zeros_like(counts)
+    cores[...] = jnp.zeros_like(cores)
+
+    def observe(c, carry):
+        at = pl.ds(pl.multiple_of(c * CHUNK, CHUNK), CHUNK)
+        local_x = obs[0:1, at] - gx * rows
+        in_y = one_hot(cols, CHUNK, obs[1:2, at] - gy * cols).astype(bf16)
+        in_z = one_hot(depth, CHUNK, obs[2:3, at]).astype(bf16)
+        in_x = [jnp.where(local_x == i, 1.0, 0.0).astype(bf16) for i in range(rows)]
+        cells = jnp.concatenate([in_y * in_x[i] for i in range(rows)], axis=0)
+        counts[...] += dot_nt(cells, in_z)
+        both = dot_nn(phiz_t, in_z)
+        high, low = split((both[:mz] + both[mz:]) * core[0:1, at])
+        weighted = jnp.concatenate(
+            [high * in_x[i] for i in range(rows)] + [low * in_x[i] for i in range(rows)], axis=0
+        )
+        cores[...] += dot_nt(weighted, in_y)
+        return carry
+
+    lax.fori_loop(0, obs.shape[1] // CHUNK, observe, 0)
+
+    loads[7].wait()
+
+    for k in (2, 3):
+        place, line = ((TILE - 1, TILE), (TILE + cols, TILE + cols - 1))[k - 2]
+
+        @pl.when(gets[k])
+        def _(k=k, place=place):
+            for field, array, scratch in fields:
                 halo(k, field, array, scratch).wait_recv()
+                scratch[1 : rows + 1, place] = arrive[k - 2, field]
 
         @pl.when(jnp.logical_not(gets[k]))
-        def _(k=k):
+        def _(place=place, line=line):
             for _, _, scratch in fields:
-                line = TILE if k == 2 else TILE + cols - 1
-                place = 0 if k == 2 else TILE + cols
-                for i in range(1, rows + 1):
-                    scratch[i, place : place + TILE] = jnp.broadcast_to(
-                        scratch[i, line : line + 1], (TILE, depth)
-                    )
+                scratch[1 : rows + 1, place] = scratch[1 : rows + 1, line]
 
     def own(scratch, i):
         return scratch[i, TILE : TILE + cols]
@@ -259,11 +254,14 @@
             device_id_type=MESH,
         )
 
+    pl.semaphore_wait(ready, n_gx - 1)
     each(peers - 1, lambda d: piece(d + 1).start())
     landed[0] = pieces[gx, gy]
     rest = landed.at[pl.ds(1, peers - 1)]
     pltpu.make_async_copy(rest, rest, piece_recv).wait()
-    out_ref[...] = jnp.sum(landed[...], axis=0)
+    total = jnp.sum(landed[...], axis=0)
+    for i in range(share_x):
+        out_ref[i] = total[:, i * mz : (i + 1) * mz]
     pltpu.make_async_copy(rest, rest, piece_send).wait()
     for k in (0, 1, 2, 3):
 
@@ -284,9 +282,9 @@
     phi_y, phi_z = phi_y.T, phi_z.T
     cores = core_values.reshape(1, seen)
     args = (pressure, adjoint, log_perm, phi_x, phi_y, phi_z, obs_cells, cores)
-    out = pl.pallas_call(
+    return pl.pallas_call(
         functools.partial(kernel, n_gx, n_gy),
-        out_shape=jax.ShapeDtypeStruct((share_y, width), f32),
+        out_shape=jax.ShapeDtypeStruct((share_x, share_y, mz), f32),
         in_specs=[pl.BlockSpec(memory_space=pltpu.HBM)] * len(args),
         out_specs=pl.BlockSpec(memory_space=pltpu.VMEM),
         scratch_shapes=[
@@ -302,6 +300,8 @@
             pltpu.VMEM((2 * rows * mz, cols), f32),
             pltpu.VMEM((rows * mz, cols), f32),
             pltpu.VMEM((2, rows * mz, mx * mz), bf16),
+            pltpu.VMEM((2, 2, rows, depth), f32),
+            pltpu.VMEM((2, 2, rows, depth), f32),
             pltpu.VMEM((n_gx, n_gy, share_y, width), f32),
             pltpu.VMEM((n_gx * n_gy, share_y, width), f32),
             pltpu.SemaphoreType.DMA((8,)),
@@ -309,12 +309,12 @@
             pltpu.SemaphoreType.DMA((8,)),
             pltpu.SemaphoreType.DMA,
             pltpu.SemaphoreType.DMA,
+            pltpu.SemaphoreType.REGULAR,
         ],
         compiler_params=pltpu.CompilerParams(
             collective_id=0, has_side_effects=True, vmem_limit_bytes=63 * 1024 * 1024
         ),
     )(*args)
-    return out.reshape(share_y, share_x, mz).transpose(1, 0, 2)
 
 
 def solution(mesh):

time: 19.9 us -> 19.8 us (level)
    reshape x2 -> x0, local copies, waits for them, and re-layouts: 1.38 us -> none  [body(): return out.reshape(share_y, share_x, mz).transpose(1, 0, 2)]
    unnamed x0 -> x1, local copies, waits for them, and re-layouts: none -> 1.38 us
where the time goes in v2:
time: 19.8 us; the launch traced here: 19.6 us
  Pallas kernels  18.3 us (92%)
  local copies, waits for them, and re-layouts  1.38 us (7%)
    pallas_call x1, Pallas kernels, body(): pl.pallas_call(functools.partial(kernel, n_gx, n_gy), out_shape=jax.Shape...  18.3 us
    unnamed x1, local copies, waits for them, and re-layouts  1.38 us

profile of v2, /device:TPU:0, one launch (start us, length us, event | category | flops | bytes accessed | tf_op | source)
XLA Modules:
  0.0 19.6 jit_solution(12105901907960815315)
XLA Ops:
  0.0 18.3 %shard_map.82 = f32[8,8,16]{2,1,0:T(8,128)} custom-call(f32[8,128,256]{2,1,0:T(8,128)} %p_in.1, f32[8,128,256]{2,1,0:T(8,128)} %a_in.1, f32[8,128,256]{2,1,0:T(8,128)} %lp_in.1, f32[8,32]{1,0:T(8,128)} %phix_in.1, f32[32,128]{1,0:T(8,128)} %bitcast.3, f32[16,256]{1,0:T(8,128)} %bitcast.4, s32[3,4096]{1,0:T(4,128)} %obs_in.1, f32[1,4096]{1,0:T(1,128)} %bitcast.5), custom_call_target="tpu_custom_call" | custom-call | tf_op jit(solution)/shard_map/pallas_call | solution.py:285
  18.3 1.4 %copy.10 = f32[8,8,16]{2,1,0:T(8,128)} copy(f32[8,8,16]{2,1,0:T(8,128)} %shard_map.82) | data formatting | bytes 8192

commit v3 on v2

--- a/solution.py
+++ b/solution.py
@@ -9,8 +9,9 @@
 
 core_weight = 100.0
 TILE = 8
-CHUNK = 512
-f32, bf16 = jnp.float32, jnp.bfloat16
+CHUNK = 2048
+f32, bf16, f8 = jnp.float32, jnp.bfloat16, jnp.float8_e4m3fn
+SLOTS = 5
 MESH = pl.DeviceIdType.MESH
 
 
@@ -79,14 +80,78 @@
     ]
     barrier = pltpu.get_barrier_semaphore()
 
-    def signal(semaphore, axis, size, d):
-        target = {axis: lax.rem(lax.axis_index(axis) + d + 1, size)}
-        pl.semaphore_signal(semaphore, inc=1, device_id=target, device_id_type=MESH)
-
-    each(n_gx - 1, functools.partial(signal, barrier, "gx", n_gx))
-    each(n_gy - 1, functools.partial(signal, barrier, "gy", n_gy))
+    sends = (gx < n_gx - 1, gx > 0, gy < n_gy - 1, gy > 0)
+    gets = (gx > 0, gx < n_gx - 1, gy > 0, gy < n_gy - 1)
+    beside = ({"gx": gx + 1}, {"gx": gx - 1}, {"gy": gy + 1}, {"gy": gy - 1})
+    neighbours = sum(jnp.where(there, 1, 0) for there in sends)
+
+    def greet(semaphore):
+        for there, target in zip(sends, beside):
+
+            @pl.when(there)
+            def _(target=target):
+                pl.semaphore_signal(semaphore, inc=1, device_id=target, device_id_type=MESH)
+
+    rounds = n_gx + n_gy - 3
+
+    def hear(i):
+        @pl.when(i < rounds)
+        def _():
+            pl.semaphore_wait(ready.at[i], neighbours)
+
+            @pl.when(i + 1 < rounds)
+            def _():
+                greet(ready.at[i + 1])
+
+    greet(barrier)
     for load in loads:
         load.start()
+
+    pl.semaphore_wait(barrier, neighbours)
+
+    own_cols = pl.ds(TILE, cols)
+
+    def halo(k, field, array, scratch):
+        src, dst = (
+            (array.at[rows - 1], scratch.at[0, own_cols]),
+            (array.at[0], scratch.at[rows + 1, own_cols]),
+            (leave.at[0, field], arrive.at[0, field]),
+            (leave.at[1, field], arrive.at[1, field]),
+        )[k]
+        return pltpu.make_async_remote_copy(
+            src_ref=src,
+            dst_ref=dst,
+            send_sem=halo_send.at[2 * k + field],
+            recv_sem=halo_recv.at[2 * k + field],
+            device_id=beside[k],
+            device_id_type=MESH,
+        )
+
+    fields = ((0, p_in, p), (1, a_in, a))
+    for k in (0, 1):
+
+        @pl.when(sends[k])
+        def _(k=k):
+            for field, array, scratch in fields:
+                halo(k, field, array, scratch).start()
+
+    loads[1].wait()
+    loads[2].wait()
+    for field, scratch in ((0, p), (1, a)):
+        leave[0, field] = scratch[1 : rows + 1, TILE + cols - 1]
+        leave[1, field] = scratch[1 : rows + 1, TILE]
+
+    for k in (2, 3):
+
+        @pl.when(sends[k])
+        def _(k=k):
+            for field, array, scratch in fields:
+                halo(k, field, array, scratch).start()
+
+    if rounds > 0:
+        greet(ready.at[0])
+    for load in loads[3:7]:
+        load.wait()
 
     loads[0].wait()
     tall, wide = rows * mz, mx * mz
@@ -108,68 +173,37 @@
     for i, half in enumerate(split(phix[...])):
         block = dot_nn(dot_nn(spread_rows, half).astype(bf16), spread_cols)
         kron[i] = jnp.where(same, block, 0.0).astype(bf16)
-    loads[1].wait()
-    loads[2].wait()
-    for field, scratch in ((0, p), (1, a)):
-        leave[0, field] = scratch[1 : rows + 1, TILE + cols - 1]
-        leave[1, field] = scratch[1 : rows + 1, TILE]
-
-    pl.semaphore_wait(barrier, n_gx + n_gy - 2)
-
-    own_cols = pl.ds(TILE, cols)
-
-    def halo(k, field, array, scratch):
-        src, dst, target = (
-            (array.at[rows - 1], scratch.at[0, own_cols], {"gx": gx + 1}),
-            (array.at[0], scratch.at[rows + 1, own_cols], {"gx": gx - 1}),
-            (leave.at[0, field], arrive.at[0, field], {"gy": gy + 1}),
-            (leave.at[1, field], arrive.at[1, field], {"gy": gy - 1}),
-        )[k]
-        return pltpu.make_async_remote_copy(
-            src_ref=src,
-            dst_ref=dst,
-            send_sem=halo_send.at[2 * k + field],
-            recv_sem=halo_recv.at[2 * k + field],
-            device_id=target,
-            device_id_type=MESH,
-        )
-
-    fields = ((0, p_in, p), (1, a_in, a))
-    sends = (gx < n_gx - 1, gx > 0, gy < n_gy - 1, gy > 0)
-    gets = (gx > 0, gx < n_gx - 1, gy > 0, gy < n_gy - 1)
-    for k in (0, 1, 2, 3):
-
-        @pl.when(sends[k])
-        def _(k=k):
-            for field, array, scratch in fields:
-                halo(k, field, array, scratch).start()
-
-    each(n_gx - 1, functools.partial(signal, ready, "gx", n_gx))
-    for load in loads[3:7]:
-        load.wait()
 
     phiz_t = stacked(phiz[...])
     phiy_t = stacked(phiy[...])
     counts[...] = jnp.zeros_like(counts)
     cores[...] = jnp.zeros_like(cores)
 
-    def observe(c, carry):
-        at = pl.ds(pl.multiple_of(c * CHUNK, CHUNK), CHUNK)
+    def observe(c):
+        at = pl.ds(c * CHUNK, CHUNK)
         local_x = obs[0:1, at] - gx * rows
         in_y = one_hot(cols, CHUNK, obs[1:2, at] - gy * cols).astype(bf16)
         in_z = one_hot(depth, CHUNK, obs[2:3, at]).astype(bf16)
         in_x = [jnp.where(local_x == i, 1.0, 0.0).astype(bf16) for i in range(rows)]
         cells = jnp.concatenate([in_y * in_x[i] for i in range(rows)], axis=0)
-        counts[...] += dot_nt(cells, in_z)
+        counts[...] += dot_nt(cells.astype(f8), in_z.astype(f8))
         both = dot_nn(phiz_t, in_z)
         high, low = split((both[:mz] + both[mz:]) * core[0:1, at])
         weighted = jnp.concatenate(
             [high * in_x[i] for i in range(rows)] + [low * in_x[i] for i in range(rows)], axis=0
         )
         cores[...] += dot_nt(weighted, in_y)
-        return carry
-
-    lax.fori_loop(0, obs.shape[1] // CHUNK, observe, 0)
+
+
+    per = -(-rounds // SLOTS)
+
+    def hear_slot(slot):
+        each(per, lambda i: hear(slot * per + i))
+
+    for c in range(obs.shape[1] // CHUNK):
+        observe(c)
+        if c < 2:
+            hear_slot(c)
 
     loads[7].wait()
 
@@ -217,6 +251,9 @@
 
     for i in range(1, rows - 1):
         project(i, flat_faces(i + 1) + x_face(i + 1, i) + x_face(i + 1, i + 2))
+        if i == rows // 2 - 1:
+            hear_slot(2)
+    hear_slot(3)
     edges = [flat_faces(1) + x_face(1, 2), flat_faces(rows) + x_face(rows, rows - 1)]
 
     for k in (0, 1):
@@ -231,6 +268,7 @@
             for _, _, scratch in fields:
                 scratch[(rows + 1) * k, TILE : TILE + cols] = own(scratch, 1 + (rows - 1) * k)
 
+    hear_slot(4)
     project(0, edges[0] + x_face(1, 0))
     project(rows - 1, edges[1] + x_face(rows, rows + 1))
 
@@ -254,7 +292,6 @@
             device_id_type=MESH,
         )
 
-    pl.semaphore_wait(ready, n_gx - 1)
     each(peers - 1, lambda d: piece(d + 1).start())
     landed[0] = pieces[gx, gy]
     rest = landed.at[pl.ds(1, peers - 1)]
@@ -309,7 +346,7 @@
             pltpu.SemaphoreType.DMA((8,)),
             pltpu.SemaphoreType.DMA,
             pltpu.SemaphoreType.DMA,
-            pltpu.SemaphoreType.REGULAR,
+            pltpu.SemaphoreType.REGULAR((max(n_gx + n_gy - 3, 1),)),
         ],
         compiler_params=pltpu.CompilerParams(
             collective_id=0, has_side_effects=True, vmem_limit_bytes=63 * 1024 * 1024

time: 19.8 us -> 19.1 us (0.965)
  Pallas kernels: 18.3 us -> 17.5 us
    pallas_call x1, Pallas kernels: 18.3 us -> 17.5 us  [body(): pl.pallas_call(functools.partial(kernel, n_gx, n_gy), out_shape=jax.Shape...]
where the time goes in v3:
time: 19.1 us; the launch traced here: 18.9 us
  Pallas kernels  17.5 us (92%)
  local copies, waits for them, and re-layouts  1.38 us (7%)
    pallas_call x1, Pallas kernels, body(): pl.pallas_call(functools.partial(kernel, n_gx, n_gy), out_shape=jax.Shape...  17.5 us
    unnamed x1, local copies, waits for them, and re-layouts  1.38 us

profile of v3, /device:TPU:0, one launch (start us, length us, event | category | flops | bytes accessed | tf_op | source)
XLA Modules:
  0.0 18.9 jit_solution(7392659539800135694)
XLA Ops:
  0.0 17.5 %shard_map.82 = f32[8,8,16]{2,1,0:T(8,128)} custom-call(f32[8,128,256]{2,1,0:T(8,128)} %p_in.1, f32[8,128,256]{2,1,0:T(8,128)} %a_in.1, f32[8,128,256]{2,1,0:T(8,128)} %lp_in.1, f32[8,32]{1,0:T(8,128)} %phix_in.1, f32[32,128]{1,0:T(8,128)} %bitcast.3, f32[16,256]{1,0:T(8,128)} %bitcast.4, s32[3,4096]{1,0:T(4,128)} %obs_in.1, f32[1,4096]{1,0:T(1,128)} %bitcast.5), custom_call_target="tpu_custom_call" | custom-call | tf_op jit(solution)/shard_map/pallas_call | solution.py:322
  17.5 1.4 %copy.10 = f32[8,8,16]{2,1,0:T(8,128)} copy(f32[8,8,16]{2,1,0:T(8,128)} %shard_map.82) | data formatting | bytes 8192

commit v4 on v3

--- a/solution.py
+++ b/solution.py
@@ -249,12 +249,13 @@
         seen = cores[top : top + mz] + cores[tall + top : tall + top + mz]
         part[at] = x + core_weight * seen
 
+    hear_slot(2)
     for i in range(1, rows - 1):
         project(i, flat_faces(i + 1) + x_face(i + 1, i) + x_face(i + 1, i + 2))
         if i == rows // 2 - 1:
-            hear_slot(2)
-    hear_slot(3)
+            hear_slot(3)
     edges = [flat_faces(1) + x_face(1, 2), flat_faces(rows) + x_face(rows, rows - 1)]
+    hear_slot(4)
 
     for k in (0, 1):
 
@@ -268,7 +269,6 @@
             for _, _, scratch in fields:
                 scratch[(rows + 1) * k, TILE : TILE + cols] = own(scratch, 1 + (rows - 1) * k)
 
-    hear_slot(4)
     project(0, edges[0] + x_face(1, 0))
     project(rows - 1, edges[1] + x_face(rows, rows + 1))
 

time: 19.1 us -> 19.1 us (level)
  no operation moved by 1% of the time
where the time goes in v4:
time: 19.1 us; the launch traced here: 18.9 us
  Pallas kernels  17.5 us (92%)
  local copies, waits for them, and re-layouts  1.38 us (7%)
    pallas_call x1, Pallas kernels, body(): pl.pallas_call(functools.partial(kernel, n_gx, n_gy), out_shape=jax.Shape...  17.5 us
    unnamed x1, local copies, waits for them, and re-layouts  1.38 us

profile of v4, /device:TPU:0, one launch (start us, length us, event | category | flops | bytes accessed | tf_op | source)
XLA Modules:
  0.0 18.9 jit_solution(6931193244938720804)
XLA Ops:
  0.0 17.5 %shard_map.82 = f32[8,8,16]{2,1,0:T(8,128)} custom-call(f32[8,128,256]{2,1,0:T(8,128)} %p_in.1, f32[8,128,256]{2,1,0:T(8,128)} %a_in.1, f32[8,128,256]{2,1,0:T(8,128)} %lp_in.1, f32[8,32]{1,0:T(8,128)} %phix_in.1, f32[32,128]{1,0:T(8,128)} %bitcast.3, f32[16,256]{1,0:T(8,128)} %bitcast.4, s32[3,4096]{1,0:T(4,128)} %obs_in.1, f32[1,4096]{1,0:T(1,128)} %bitcast.5), custom_call_target="tpu_custom_call" | custom-call | tf_op jit(solution)/shard_map/pallas_call | solution.py:322
  17.5 1.4 %copy.10 = f32[8,8,16]{2,1,0:T(8,128)} copy(f32[8,8,16]{2,1,0:T(8,128)} %shard_map.82) | data formatting | bytes 8192
